TPU v7x, 32 devices: a whole 2x2x4 slice. The times are simulated.
32 devices in a mesh: tm: 4 (over y, x), height: 4 (over z), width: 2 (over core).
Axes of the slice: x: 2, y: 2, z: 4, core: 2. Of those that a mesh axis runs over, the one named last changes fastest.
Arguments:
- video: bfloat16 [64, 64, 32, 256], P('tm', 'height', 'width'), may hold values from -12 to 12
- w_space: bfloat16 [3, 3, 256, 256], replicated, may hold values from -0.125 to 0.125
- w_time: bfloat16 [3, 256, 256], replicated, may hold values from -0.21875 to 0.21875
- norm_gain: float32 [256], replicated, may hold values from 0.1 to 1.9
- norm_bias: float32 [256], replicated, may hold values from -1 to 1
- w_qkv: bfloat16 [256, 768], replicated, may hold values from -64 to 64
- w_out: bfloat16 [256, 256], replicated, may hold values from -0.375 to 0.375
Outputs:
- block_out: bfloat16 [64, 64, 32, 256], P('tm', 'height', 'width')
All inputs are finite; a program needn't handle non-finite values.
Results may differ from a plain program's by a relative error of at most 0.012.
Values may be sent and summed in bfloat16 or wider, within the bound.
A program may use at most 128 MiB of HBM per device.

v0:
```python
import math

import jax
import jax.numpy as jnp
from jax import lax
from jax.sharding import PartitionSpec as P

HEADS = 8
GROUPS = 32


def padded_2(value, sides, width):
    for axis, dim in sides:
        size, length = (lax.axis_size(axis), value.shape[dim])
        up = [(i, (i + 1) % size) for i in range(size - 1)]
        down = [(j, i) for i, j in up]
        last = lax.slice_in_dim(value, length - width, length, axis=dim)
        first = lax.slice_in_dim(value, 0, width, axis=dim)
        before = lax.ppermute(last, axis, up)
        after = lax.ppermute(first, axis, down)
        value = jnp.concatenate([before, value, after], axis=dim)
    return value


def attend(block, w_qkv, w_out):
    frames, pixels, channels = block.shape
    head_size = channels // HEADS
    flattened = block.reshape(frames * pixels, channels)
    projected = jnp.dot(flattened, w_qkv, preferred_element_type=jnp.float32).astype(jnp.bfloat16)
    projected = projected.reshape(frames, pixels, 3, HEADS, head_size)
    scores = jnp.einsum(
        "fphd,gphd->phfg",
        projected[:, :, 0],
        projected[:, :, 1],
        preferred_element_type=jnp.float32,
    ) / math.sqrt(head_size)
    weights = jax.nn.softmax(scores, axis=-1).astype(jnp.bfloat16)
    context = jnp.einsum(
        "phfg,gphd->fphd", weights, projected[:, :, 2], preferred_element_type=jnp.float32
    ).astype(jnp.bfloat16)
    context = context.reshape(frames * pixels, channels)
    result = flattened.astype(jnp.float32) + jnp.dot(
        context, w_out, preferred_element_type=jnp.float32
    )
    return result.reshape(frames, pixels, channels).astype(jnp.bfloat16)


def attend_slot(block, w_qkv, w_out):
    return attend(block[:, 0], w_qkv, w_out)[:, None]


def per_device(video, w_space, w_time, norm_gain, norm_bias, w_qkv, w_out):
    frames, rows, cols, channels = video.shape
    pixels = rows * cols
    padded = padded_2(video, (("height", 1), ("width", 2)), 1)
    running = jnp.zeros((frames * pixels, channels), jnp.float32)
    for row_step in range(3):
        for col_step in range(3):
            window_piece = padded[
                :, row_step : row_step + rows, col_step : col_step + cols
            ].reshape(frames * pixels, channels)
            running = running + jnp.dot(
                window_piece, w_space[row_step, col_step], preferred_element_type=jnp.float32
            )
    spatial = running.reshape(frames, pixels, channels).astype(jnp.bfloat16)
    framed = padded_2(spatial, (("tm", 0),), 1)
    running = spatial.astype(jnp.float32).reshape(frames * pixels, channels)
    for tap in range(3):
        running = running + jnp.dot(
            framed[tap : tap + frames].reshape(frames * pixels, channels),
            w_time[tap],
            preferred_element_type=jnp.float32,
        )
    temporal = running.astype(jnp.bfloat16)
    grouped = temporal.astype(jnp.float32).reshape(frames * pixels, GROUPS, channels // GROUPS)
    cell_count = float(
        frames
        * lax.axis_size("tm")
        * rows
        * lax.axis_size("height")
        * cols
        * lax.axis_size("width")
        * (channels // GROUPS)
    )
    local_sum = jnp.sum(grouped, axis=(0, 2))
    total_sum, total_square = lax.psum(
        (local_sum, jnp.sum(grouped * grouped, axis=(0, 2))), ("tm", "height", "width")
    )
    group_mean = total_sum / cell_count
    group_var = jnp.maximum(total_square / cell_count - group_mean * group_mean, 0.0)
    centered = grouped - group_mean[None, :, None]
    scaled = centered * lax.rsqrt(group_var + 1e-05)[None, :, None]
    scaled = scaled.reshape(frames * pixels, channels) * norm_gain + norm_bias
    normed = jax.nn.silu(scaled).astype(jnp.bfloat16).reshape(frames, pixels, channels)
    tm_count = lax.axis_size("tm")
    slotted = normed.reshape(frames, tm_count, pixels // tm_count, channels)
    outcome = (lambda block: attend_slot(block, w_qkv, w_out))(
        lax.all_to_all(slotted, "tm", split_axis=1, concat_axis=0, tiled=True)
    )
    result = lax.all_to_all(outcome, "tm", split_axis=0, concat_axis=1, tiled=True)
    return result.reshape(frames, rows, cols, channels)


def solution(mesh):
    placed = (P("tm", "height", "width", None), P(), P(), P(), P(), P(), P())
    return jax.shard_map(
        per_device,
        mesh=mesh,
        in_specs=placed,
        out_specs=P("tm", "height", "width", None),
        check_vma=False,
    )
```

profile of v0, /device:TPU:0, one launch (start us, length us, event | category | flops | bytes accessed | tf_op | source)
XLA Modules:
  0.0 266.4 jit_solution(11430516344102743001)
XLA Ops:
  0.0 1.0 fusion.61
  1.0 4.9 %collective-permute-start = (bf16[16,1,16,256]{3,2,1,0:T(8,128)(2,1)S(1)}, bf16[16,1,16,256]{3,2,1,0:T(8,128)(2,1)S(1)}, u32[]{:S(2)}, u32[]{:S(2)}) collective-permute-start(bf16[16,1,16,256]{3,2,1,0:T(8,128)(2,1)S(1)} %get-tuple-element.31), channel_id=1, source_target_pairs={{0,2},{2,4},{4,6},{1,3},{3,5},{5,7},{8,10},{10,12},{12,14},{9,11},... | collective-permute-start | bytes 393224 | tf_op jit(solution)/shard_map/ppermute | solution.py:19
  6.0 1.3 collective-permute-start.1
  7.3 1.4 collective-permute-done
  8.7 4.1 %collective-permute-done.1 = bf16[16,1,16,256]{3,2,1,0:T(8,128)(2,1)S(1)} collective-permute-done((bf16[16,1,16,256]{3,2,1,0:T(8,128)(2,1)S(1)}, bf16[16,1,16,256]{3,2,1,0:T(8,128)(2,1)S(1)}, u32[]{:S(2)}, u32[]{:S(2)}) %collective-permute-start.1) | collective-permute-done | bytes 131104 | tf_op jit(solution)/shard_map/ppermute | solution.py:20
  12.9 3.3 %pad_maximum_fusion.3 = (bf16[16,16,16,256]{3,2,1,0:T(8,128)(2,1)S(1)}, bf16[16,18,16,256]{3,2,1,0:T(8,128)(2,1)S(1)}, bf16[16,16,16,256]{3,2,1,0:T(8,128)(2,1)S(1)}) fusion(bf16[16,1,16,256]{3,2,1,0:T(8,128)(2,1)S(1)} %collective-permute-done.1, bf16[16,16,16,256]{3,2,1,0:T(8,128)(2,1)} %param.7, ...), kind=kLoop, calls=%fused_computation.56 | loop fusion | flops 8388608 | bytes 8650752 | tf_op jit(solution)/shard_map/concatenate | solution.py:21
  16.2 0.5 fusion.60
  16.7 1.3 collective-permute-start.3
  18.0 3.0 %collective-permute-start.2 = (bf16[16,18,1,256]{3,0,2,1:T(8,128)(2,1)S(1)}, bf16[16,18,1,256]{3,0,2,1:T(8,128)(2,1)S(1)}, u32[]{:S(2)}, u32[]{:S(2)}) collective-permute-start(bf16[16,18,1,256]{3,0,2,1:T(8,128)(2,1)S(1)} %copy.36), channel_id=1, source_target_pairs={{0,1},{2,3},{4,5},{6,7},{8,9},{10,11},{12,13},{14,15},{16,17},{18,... | collective-permute-start | bytes 442376 | tf_op jit(solution)/shard_map/ppermute | solution.py:19
  21.0 0.2 copy.39
  21.3 0.7 collective-permute-done.2
  22.0 0.2 copy.37
  22.2 0.0 copy-start.3
  22.3 7.0 %pad_maximum_fusion.4 = (bf16[16,16,16,256]{3,2,1,0:T(8,128)(2,1)S(1)}, bf16[16,16,16,256]{3,2,1,0:T(8,128)(2,1)S(1)}, bf16[16,16,16,256]{3,2,1,0:T(8,128)(2,1)S...) fusion(bf16[16,18,16,256]{3,2,1,0:T(8,128)(2,1)S(1)} %constant_, ...), kind=kLoop, calls=%fused_computation.57 | loop fusion | flops 25165824 | bytes 15237120 | tf_op jit(solution)/shard_map/concatenate | solution.py:21
  29.3 0.7 fusion.44
  30.0 0.7 fusion.35
  30.7 0.7 convolution_add_fusion.9
  31.5 0.8 convolution_add_fusion.8
  32.2 0.0 copy-start.2
  32.2 0.7 convolution_add_fusion.7
  33.0 0.9 copy-done.2
  33.8 0.8 convolution_add_fusion.6
  34.6 0.8 convolution_add_fusion.5
  35.4 0.7 convolution_add_fusion.4
  36.1 0.0 copy-start.4
  36.1 0.9 fusion.10
  37.0 1.3 collective-permute-start.5
  38.3 4.7 %collective-permute-start.4 = (bf16[1,256,256]{2,1,0:T(8,128)(2,1)S(1)}, bf16[1,256,256]{2,1,0:T(8,128)(2,1)S(1)}, u32[]{:S(2)}, u32[]{:S(2)}) collective-permute-start(bf16[1,256,256]{2,1,0:T(8,128)(2,1)S(1)} %get-tuple-element.26), channel_id=1, source_target_pairs={{0,8},{8,16},{16,24},{1,9},{9,17},{17,25},{2,10},{10,18},{18,26},{... | collective-permute-start | bytes 393224 | tf_op jit(solution)/shard_map/ppermute | solution.py:19
  43.1 0.7 fusion.32
  43.8 0.9 collective-permute-done.5
  44.7 1.2 collective-permute-done.4
  45.8 0.4 pad_maximum_fusion
  46.2 0.7 fusion.6
  46.9 0.0 copy-start.6
  46.9 0.0 copy-start.7
  47.0 1.0 convert_reduce_fusion
  48.0 0.1 reduce_sum.32
  48.1 0.1 reduce_sum.45
  48.1 0.1 reduce_sum.36
  48.3 0.1 reduce_sum.46
  48.4 42.1 %all-reduce = (f32[32]{0:T(128)S(1)}, f32[32]{0:T(128)S(1)}) all-reduce(f32[32]{0:T(128)S(1)} %reduce_sum.46, f32[32]{0:T(128)S(1)} %reduce_sum.36), channel_id=1, replica_groups=mesh['tm'=4,'height'=4,'width'=2] {'tm','height','width'}, use_global_device_ids=true, to_apply=%region_5.6 | all-reduce | flops 64 | bytes 512 | tf_op jit(solution)/shard_map/psum | solution.py:86
  90.5 0.1 sub.24
  90.5 0.1 sub.25
  90.6 0.1 mul.34
  90.7 0.1 mul.35
  90.8 1.4 fusion.19
  92.3 0.2 copy.40
  92.5 28.2 %all_to_all.30 = bf16[16,4,64,256]{3,2,0,1:T(8,128)(2,1)S(1)} all-to-all(bf16[16,4,64,256]{3,2,0,1:T(8,128)(2,1)S(1)} %copy.40), channel_id=1, replica_groups=mesh['tm'=4,'height'=4,'width'=2] {'tm'}, dimensions={1} | all-to-all | bytes 4194304 | tf_op jit(solution)/shard_map/all_to_all | solution.py:98
  120.7 4.5 %convolution_convert_fusion = bf16[4096,768]{1,0:T(8,128)(2,1)} fusion(bf16[4096,256]{1,0:T(8,128)(2,1)S(1)} %bitcast.103, bf16[256,768]{1,0:T(8,128)(2,1)S(1)} %copy-done), kind=kOutput, calls=%fused_computation.7 | convolution fusion | flops 1613758464 | bytes 8781824 | tf_op jit(solution)/shard_map/dot_general | solution.py:29
  125.2 8.6 %copy.41 = bf16[4096,768]{0,1:T(8,128)(2,1)} copy(bf16[4096,768]{1,0:T(8,128)(2,1)} %convolution_convert_fusion) | data formatting | bytes 12582912 | tf_op jit(solution)/shard_map/convert_element_type | solution.py:29
  133.7 17.9 %reshape.85 = bf16[64,64,3,8,32]{1,0,4,3,2:T(8,128)(2,1)} reshape(bf16[4096,768]{0,1:T(8,128)(2,1)} %copy.41) | data formatting | bytes 12582912 | tf_op jit(solution)/shard_map/reshape | solution.py:30
  151.7 9.3 %fusion.59 = (bf16[64,64,1,8,32]{1,0,4,3,2:T(8,128)(2,1)}, bf16[64,64,1,8,32]{1,0,4,3,2:T(8,128)(2,1)}, bf16[64,64,1,8,32]{1,0,4,3,2:T(8,128)(2,1)}) fusion(bf16[64,64,3,8,32]{1,0,4,3,2:T(8,128)(2,1)} %reshape.85), kind=kLoop, calls=%fused_computation.94 | loop fusion | bytes 12582912 | tf_op jit(solution)/shard_map/slice | solution.py:39
  161.0 7.2 %copy.50 = bf16[64,64,1,8,32]{0,4,3,1,2:T(8,128)(2,1)} copy(bf16[64,64,1,8,32]{1,0,4,3,2:T(8,128)(2,1)} %get-tuple-element.9) | data formatting | bytes 4194304
  168.2 7.2 %copy.51 = bf16[64,64,1,8,32]{0,4,3,1,2:T(8,128)(2,1)} copy(bf16[64,64,1,8,32]{1,0,4,3,2:T(8,128)(2,1)} %get-tuple-element.10) | data formatting | bytes 4194304
  175.3 7.2 %copy.52 = bf16[64,64,1,8,32]{0,4,3,1,2:T(8,128)(2,1)} copy(bf16[64,64,1,8,32]{1,0,4,3,2:T(8,128)(2,1)} %get-tuple-element.11) | data formatting | bytes 4194304
  182.5 11.6 %fusion.21 = f32[64,8,64,64]{2,3,1,0:T(8,128)} fusion(bf16[64,64,1,8,32]{0,4,3,1,2:T(8,128)(2,1)} %copy.52, bf16[64,64,1,8,32]{0,4,3,1,2:T(8,128)(2,1)} %copy.51), kind=kOutput, calls=%fused_computation.40 | convolution fusion | flops 134217728 | bytes 12582912 | tf_op jit(solution)/shard_map/fphd,gphd->phfg/dot_general | solution.py:31
  194.2 18.4 %fusion.62 = (f32[64,8,64]{2,1,0:T(8,128)S(1)}, f32[64,8,64,64]{2,3,1,0:T(8,128)}) fusion(f32[64,8,64,64]{2,3,1,0:T(8,128)} %fusion.21), kind=kOutput, calls=%fused_computation.97 | output fusion | flops 8388671 | bytes 16908288 | tf_op jit(solution)/shard_map/sub | solution.py:37
  212.6 11.3 %convert_bitcast_fusion = bf16[64,64,8,32]{0,3,2,1:T(8,128)(2,1)} fusion(f32[64,8,64,64]{2,3,1,0:T(8,128)} %get-tuple-element.36, f32[64,8,64]{2,1,0:T(8,128)S(1)} %get-tuple-element.35, bf16[64,64,1,8,32]{0,4,3,1,2:T(8,128)(2,1)} %copy.50), kind=kOutput, calls=%fused_computation.44 | convolution fusion | flops 139460608 | bytes 12713984 | tf_op jit(solution)/shard_map/phfg,gphd->fphd/dot_general | solution.py:38
  223.9 7.2 %copy.46 = bf16[64,64,8,32]{1,0,3,2:T(8,128)(2,1)} copy(bf16[64,64,8,32]{0,3,2,1:T(8,128)(2,1)} %convert_bitcast_fusion) | data formatting | bytes 4194304 | tf_op jit(solution)/shard_map/convert_element_type | solution.py:40
  231.1 6.6 %reshape.86 = bf16[4096,256]{0,1:T(8,128)(2,1)} reshape(bf16[64,64,8,32]{1,0,3,2:T(8,128)(2,1)} %copy.46) | data formatting | bytes 4194304 | tf_op jit(solution)/shard_map/reshape | solution.py:41
  237.7 2.3 fusion.9
  240.1 0.0 copy-start.1
  240.1 24.8 %all_to_all.31 = bf16[64,1,64,256]{3,2,1,0:T(8,128)(2,1)S(1)} all-to-all(bf16[64,1,64,256]{3,2,1,0:T(8,128)(2,1)S(1)} %bitcast.110), channel_id=1, replica_groups=mesh['tm'=4,'height'=4,'width'=2] {'tm'}, dimensions={0} | all-to-all | bytes 4194304 | tf_op jit(solution)/shard_map/all_to_all | solution.py:100
  264.9 1.5 copy.48
  (16 shorter events, 0.1 us)
Async XLA Ops:
  0.0 120.7 %copy-start = (bf16[256,768]{1,0:T(8,128)(2,1)S(1)}, bf16[256,768]{1,0:T(8,128)(2,1)}, u32[]{:S(2)}) copy-start(bf16[256,768]{1,0:T(8,128)(2,1)} %param.12) | copy-start | bytes 1179652
  1.0 7.7 %collective-permute-start = (bf16[16,1,16,256]{3,2,1,0:T(8,128)(2,1)S(1)}, bf16[16,1,16,256]{3,2,1,0:T(8,128)(2,1)S(1)}, u32[]{:S(2)}, u32[]{:S(2)}) collective-permute-start(bf16[16,1,16,256]{3,2,1,0:T(8,128)(2,1)S(1)} %get-tuple-element.31), channel_id=1, source_target_pairs={{0,2},{2,4},{4,6},{1,3},{3,5},{5,7},{8,10},{10,12},{12,14},{9,11},... | collective-permute-start | bytes 393224 | tf_op jit(solution)/shard_map/ppermute | solution.py:19
  6.0 6.9 %collective-permute-start.1 = (bf16[16,1,16,256]{3,2,1,0:T(8,128)(2,1)S(1)}, bf16[16,1,16,256]{3,2,1,0:T(8,128)(2,1)S(1)}, u32[]{:S(2)}, u32[]{:S(2)}) collective-permute-start(bf16[16,1,16,256]{3,2,1,0:T(8,128)(2,1)S(1)} %get-tuple-element.30), channel_id=1, source_target_pairs={{2,0},{4,2},{6,4},{3,1},{5,3},{7,5},{10,8},{12,10},{14,12},{11,9},... | collective-permute-start | bytes 393224 | tf_op jit(solution)/shard_map/ppermute | solution.py:20
  16.7 4.4 %collective-permute-start.3 = (bf16[16,18,1,256]{3,0,2,1:T(8,128)(2,1)S(1)}, bf16[16,18,1,256]{3,0,2,1:T(8,128)(2,1)S(1)}, u32[]{:S(2)}, u32[]{:S(2)}) collective-permute-start(bf16[16,18,1,256]{3,0,2,1:T(8,128)(2,1)S(1)} %copy.38), channel_id=1, source_target_pairs={{1,0},{3,2},{5,4},{7,6},{9,8},{11,10},{13,12},{15,14},{17,16},{19,... | collective-permute-start | bytes 442376 | tf_op jit(solution)/shard_map/ppermute | solution.py:20
  18.0 4.0 %collective-permute-start.2 = (bf16[16,18,1,256]{3,0,2,1:T(8,128)(2,1)S(1)}, bf16[16,18,1,256]{3,0,2,1:T(8,128)(2,1)S(1)}, u32[]{:S(2)}, u32[]{:S(2)}) collective-permute-start(bf16[16,18,1,256]{3,0,2,1:T(8,128)(2,1)S(1)} %copy.36), channel_id=1, source_target_pairs={{0,1},{2,3},{4,5},{6,7},{8,9},{10,11},{12,13},{14,15},{16,17},{18,... | collective-permute-start | bytes 442376 | tf_op jit(solution)/shard_map/ppermute | solution.py:19
  22.2 7.1 %copy-start.3 = (bf16[3,3,256,256]{3,2,1,0:T(8,128)(2,1)S(1)}, bf16[3,3,256,256]{3,2,1,0:T(8,128)(2,1)}, u32[]{:S(2)}) copy-start(bf16[3,3,256,256]{3,2,1,0:T(8,128)(2,1)} %param.8) | copy-start | bytes 3538948
  32.2 1.6 copy-start.2
  36.1 7.0 %copy-start.4 = (bf16[3,256,256]{2,1,0:T(8,128)(2,1)S(1)}, bf16[3,256,256]{2,1,0:T(8,128)(2,1)}, u32[]{:S(2)}) copy-start(bf16[3,256,256]{2,1,0:T(8,128)(2,1)} %param.9) | copy-start | bytes 1179652
  37.0 7.7 %collective-permute-start.5 = (bf16[1,256,256]{2,1,0:T(8,128)(2,1)S(1)}, bf16[1,256,256]{2,1,0:T(8,128)(2,1)S(1)}, u32[]{:S(2)}, u32[]{:S(2)}) collective-permute-start(bf16[1,256,256]{2,1,0:T(8,128)(2,1)S(1)} %get-tuple-element.25), channel_id=1, source_target_pairs={{8,0},{16,8},{24,16},{9,1},{17,9},{25,17},{10,2},{18,10},{26,18},{... | collective-permute-start | bytes 393224 | tf_op jit(solution)/shard_map/ppermute | solution.py:20
  38.3 7.5 %collective-permute-start.4 = (bf16[1,256,256]{2,1,0:T(8,128)(2,1)S(1)}, bf16[1,256,256]{2,1,0:T(8,128)(2,1)S(1)}, u32[]{:S(2)}, u32[]{:S(2)}) collective-permute-start(bf16[1,256,256]{2,1,0:T(8,128)(2,1)S(1)} %get-tuple-element.26), channel_id=1, source_target_pairs={{0,8},{8,16},{16,24},{1,9},{9,17},{17,25},{2,10},{10,18},{18,26},{... | collective-permute-start | bytes 393224 | tf_op jit(solution)/shard_map/ppermute | solution.py:19
  46.9 43.9 %copy-start.6 = (f32[256]{0:T(256)S(1)}, f32[256]{0:T(256)}, u32[]{:S(2)}) copy-start(f32[256]{0:T(256)} %param.11) | copy-start | bytes 3076
  46.9 43.9 %copy-start.7 = (f32[256]{0:T(256)S(1)}, f32[256]{0:T(256)}, u32[]{:S(2)}) copy-start(f32[256]{0:T(256)} %param.10) | copy-start | bytes 3076
  231.1 6.7 %copy-start.5 = (bf16[256,256]{1,0:T(8,128)(2,1)S(1)}, bf16[256,256]{1,0:T(8,128)(2,1)}, u32[]{:S(2)}) copy-start(bf16[256,256]{1,0:T(8,128)(2,1)} %param.13) | copy-start | bytes 393220
  240.1 26.3 %copy-start.1 = (bf16[256,768]{1,0:T(8,128)(2,1)S(1)}, bf16[256,768]{1,0:T(8,128)(2,1)}, u32[]{:S(2)}) copy-start(bf16[256,768]{1,0:T(8,128)(2,1)} %param.12) | copy-start | bytes 1179652
where the time goes:
time: 268 us; the launch traced here: 266 us
  blocking collectives  95.1 us (35%)
  local copies, waits for them, and re-layouts  76.4 us (29%)
  matrix products  38.9 us (15%)
  other arithmetic  30.8 us (11%)
  starting transfers between devices  16.6 us (6%)
  waiting for transfers between devices  8.35 us (3%)
    psum x1, blocking collectives, per_device(): lax.psum((local_sum, jnp.sum(grouped * grouped, axis=(0, 2))), ('tm', 'he...  42.1 us
    all_to_all x1, blocking collectives, per_device(): lax.all_to_all(slotted, 'tm', split_axis=1, concat_axis=0, tiled=True)  28.2 us
    all_to_all x1, blocking collectives, per_device(): lax.all_to_all(outcome, 'tm', split_axis=0, concat_axis=1, tiled=True)  24.8 us
    unnamed x20, local copies, waits for them, and re-layouts  22.5 us
    sub x1, other arithmetic, attend(): weights = jax.nn.softmax(scores, axis=-1).astype(jnp.bfloat16)  18.4 us
    reshape x1, local copies, waits for them, and re-layouts, attend(): projected = projected.reshape(frames, pixels, 3, HEADS, head_size)  17.9 us
    ppermute x3, starting transfers between devices, padded_2(): before = lax.ppermute(last, axis, up)  12.7 us
    dot_general x1, matrix products, attend(): jnp.einsum('fphd,gphd->phfg', projected[:, :, 0], projected[:, :, 1], pre...  11.6 us
  transfers between devices with their start and end apart: 6, of which 5 were waited for; matrix products, arithmetic and copies ran while one was open for 0% of the time, Pallas kernels for 0%

commit v1 on v0

v1 whole, which is shorter than its diff:
```python
import functools
import math

import jax
import jax.numpy as jnp
from jax import lax
from jax.experimental import pallas as pl
from jax.experimental.pallas import tpu as pltpu
from jax.sharding import PartitionSpec as P

HEADS = 8
GROUPS = 32
EPS = 1e-5
MESH = pl.DeviceIdType.MESH
STEPS = [(dr, dc) for dr in (-1, 0, 1) for dc in (-1, 0, 1) if (dr, dc) != (0, 0)]


def dot(a, b):
    return jnp.dot(a, b, preferred_element_type=jnp.float32)


def inside(index, size):
    return jnp.logical_and(index >= 0, index < size)


def kernel(
    sizes, x_ref, wsp_ref, wt_ref, gain_ref, bias_ref, wqkv_ref, wout_ref, out_ref,
    pad, spat, edge_out, edge_in, tmp, piece, recv, stage, qkv, ctx, normed_buf,
    stat, ex_t, ex_h, ex_w,
    load_sem, halo_send, halo_recv, edge_send, edge_recv, fwd_send, fwd_recv,
    back_send, back_recv, t_send, t_recv, h_send, h_recv, w_send, w_recv,
):
    nt, nh, nw = sizes
    rows, cols, frames, channels = x_ref.shape
    span = rows // nt
    unit = cols * frames
    total = nt * frames
    head = channels // HEADS
    t, h, w = (lax.axis_index(name) for name in ("tm", "height", "width"))

    barrier = pltpu.get_barrier_semaphore()
    count = 0
    for dr, dc in STEPS:
        there = jnp.logical_and(inside(h + dr, nh), inside(w + dc, nw))

        @pl.when(there)
        def _(dr=dr, dc=dc):
            pl.semaphore_signal(barrier, inc=1, device_id=(t, h + dr, w + dc), device_id_type=MESH)

        count = count + there.astype(jnp.int32)
    for k in range(1, nt):
        pl.semaphore_signal(barrier, inc=1, device_id=(lax.rem(t + k, nt), h, w), device_id_type=MESH)
    for k in range(1, nh):
        pl.semaphore_signal(barrier, inc=1, device_id=(t, lax.rem(h + k, nh), w), device_id_type=MESH)
    for k in range(1, nw):
        pl.semaphore_signal(barrier, inc=1, device_id=(t, h, lax.rem(w + k, nw)), device_id_type=MESH)

    load = pltpu.make_async_copy(x_ref, pad.at[pl.ds(1, rows), pl.ds(1, cols)], load_sem)
    load.start()
    pl.semaphore_wait(barrier, count + (nt - 1) + (nh - 1) + (nw - 1))

    def span_of(step, size):
        src = {-1: pl.ds(0, 1), 0: pl.ds(0, size), 1: pl.ds(size - 1, 1)}[step]
        dst = {-1: pl.ds(size + 1, 1), 0: pl.ds(1, size), 1: pl.ds(0, 1)}[step]
        return src, dst

    def halo(index, sign):
        dr, dc = STEPS[index]
        (src_r, dst_r), (src_c, dst_c) = span_of(dr, rows), span_of(dc, cols)
        return pltpu.make_async_remote_copy(
            src_ref=x_ref.at[src_r, src_c], dst_ref=pad.at[dst_r, dst_c],
            send_sem=halo_send.at[index], recv_sem=halo_recv.at[index],
            device_id=(t, h + sign * dr, w + sign * dc), device_id_type=MESH,
        )

    for index, (dr, dc) in enumerate(STEPS):
        @pl.when(jnp.logical_and(inside(h + dr, nh), inside(w + dc, nw)))
        def _(index=index):
            halo(index, 1).start()
    for index, (dr, dc) in enumerate(STEPS):
        @pl.when(jnp.logical_not(jnp.logical_and(inside(h - dr, nh), inside(w - dc, nw))))
        def _(dr=dr, dc=dc):
            dst_r, dst_c = span_of(dr, rows)[1], span_of(dc, cols)[1]
            pad[dst_r, dst_c] = jnp.zeros((dst_r.size, dst_c.size, frames, channels), pad.dtype)
    load.wait()
    for index, (dr, dc) in enumerate(STEPS):
        @pl.when(jnp.logical_and(inside(h - dr, nh), inside(w - dc, nw)))
        def _(index=index):
            halo(index, -1).wait_recv()

    block = 2 if rows % 2 == 0 else 1

    def conv_step(step, carry):
        r = step * block
        acc = jnp.zeros((block * unit, channels), jnp.float32)
        for i in range(3):
            for j in range(3):
                taps = pad[pl.ds(r + i, block), pl.ds(j, cols)].reshape(block * unit, channels)
                acc = acc + dot(taps, wsp_ref[i, j])
        value = acc.astype(jnp.bfloat16)
        spat[pl.ds(r, block)] = value.reshape(block, unit, channels)
        lanes = tmp.shape[2]
        for c in range(channels // lanes):
            tmp[c] = value[:, c * lanes:(c + 1) * lanes].astype(jnp.float32)
        for b in range(block):
            for side, frame in ((0, 0), (1, frames - 1)):
                edge_out[side, r + b] = jnp.concatenate(
                    [tmp[c, pl.ds(b * unit + frame, cols, stride=frames), :]
                     for c in range(channels // lanes)], axis=1
                ).astype(jnp.bfloat16)
        return carry

    lax.fori_loop(0, rows // block, conv_step, 0)

    def edge(side, sign):
        step = (-1, 1)[side]
        return pltpu.make_async_remote_copy(
            src_ref=edge_out.at[side], dst_ref=edge_in.at[side],
            send_sem=edge_send.at[side], recv_sem=edge_recv.at[side],
            device_id=(t + sign * step, h, w), device_id_type=MESH,
        )

    for side, step in ((0, -1), (1, 1)):
        @pl.when(inside(t + step, nt))
        def _(side=side):
            edge(side, 1).start()

        @pl.when(jnp.logical_not(inside(t - step, nt)))
        def _(side=side):
            edge_in[side] = jnp.zeros(edge_in.shape[1:], edge_in.dtype)
    for side, step in ((0, -1), (1, 1)):
        @pl.when(inside(t - step, nt))
        def _(side=side):
            edge(side, -1).wait_recv()

    stat[...] = jnp.zeros_like(stat)
    frame_of = lax.rem(lax.broadcasted_iota(jnp.int32, (unit, channels), 0), frames)

    def forward(k, s):
        to = lax.rem(t + k, nt)
        return pltpu.make_async_remote_copy(
            src_ref=piece.at[k, s], dst_ref=recv.at[t, s],
            send_sem=fwd_send.at[k, s], recv_sem=fwd_recv.at[k, s],
            device_id=(to, h, w), device_id_type=MESH,
        )

    def time_step(s, carry):
        for k in list(range(1, nt)) + [0]:
            r = lax.rem(t + k, nt) * span + s
            here = spat[r]
            before = pltpu.roll(dot(here, wt_ref[0]), 1, 0)
            after = pltpu.roll(dot(here, wt_ref[2]), unit - 1, 0)
            spread = lambda v: jnp.broadcast_to(v[:, None, :], (cols, frames, channels)).reshape(unit, channels)
            first = spread(dot(edge_in[1, r], wt_ref[0]))
            last = spread(dot(edge_in[0, r], wt_ref[2]))
            value = here.astype(jnp.float32) + dot(here, wt_ref[1])
            value = value + jnp.where(frame_of == 0, first, before)
            value = value + jnp.where(frame_of == frames - 1, last, after)
            value = value.astype(jnp.bfloat16)
            if k:
                piece[k, s] = value
                forward(k, s).start()
            else:
                recv[t, s] = value
            wide = value.astype(jnp.float32)
            stat[0:1] += jnp.sum(wide, axis=0, keepdims=True)
            stat[1:2] += jnp.sum(wide * wide, axis=0, keepdims=True)
        return carry

    lax.fori_loop(0, span, time_step, 0)

    def exchange(slots, size, me, device, send, arrive):
        slots[me] = stat[...]

        def copy(k):
            return pltpu.make_async_remote_copy(
                src_ref=slots.at[me], dst_ref=slots.at[me],
                send_sem=send.at[k], recv_sem=arrive.at[k],
                device_id=device(lax.rem(me + k, size)), device_id_type=MESH,
            )

        def landed(k):
            other = lax.rem(me + size - k, size)
            return pltpu.make_async_remote_copy(
                src_ref=slots.at[other], dst_ref=slots.at[other],
                send_sem=send.at[k], recv_sem=arrive.at[k],
                device_id=device(other), device_id_type=MESH,
            )

        for k in range(1, size):
            copy(k).start()
        for k in range(1, size):
            landed(k).wait_recv()
        stat[...] = jnp.sum(slots[...], axis=0)
        for k in range(1, size):
            copy(k).wait_send()

    exchange(ex_t, nt, t, lambda o: (o, h, w), t_send, t_recv)
    exchange(ex_h, nh, h, lambda o: (t, o, w), h_send, h_recv)
    exchange(ex_w, nw, w, lambda o: (t, h, o), w_send, w_recv)

    cells = float(total * rows * nh * cols * nw * (channels // GROUPS))
    size = channels // GROUPS
    same = (
        lax.broadcasted_iota(jnp.int32, (channels, channels), 0) // size
        == lax.broadcasted_iota(jnp.int32, (channels, channels), 1) // size
    ).astype(jnp.float32)
    sums = jnp.dot(
        stat[...], same, precision=lax.Precision.HIGHEST, preferred_element_type=jnp.float32
    ) / cells
    mean = sums[0:1]
    var = jnp.maximum(sums[1:2] - mean * mean, 0.0)
    gain = lax.rsqrt(var + EPS) * gain_ref[...]
    bias = bias_ref[...]

    lane_head = lax.broadcasted_iota(jnp.int32, (total, channels), 1) // head
    factor = math.log2(math.e) / math.sqrt(head)

    def back(k, s):
        to = lax.rem(t + k, nt)
        return pltpu.make_async_remote_copy(
            src_ref=stage.at[to, s], dst_ref=out_ref.at[t, s],
            send_sem=back_send.at[k, s], recv_sem=back_recv.at[k, s],
            device_id=(to, h, w), device_id_type=MESH,
        )

    def attend_unit(s, carry):
        for k in range(1, nt):
            forward(k, s).wait_recv()
        for i in range(nt):
            v = (recv[i, s].astype(jnp.float32) - mean) * gain + bias
            v = (v / (1.0 + jnp.exp(-v))).astype(jnp.bfloat16)
            normed_buf[:, i * frames:(i + 1) * frames] = v.reshape(cols, frames, channels)
        rows_in = normed_buf[...].reshape(cols * total, channels)
        qkv[...] = dot(rows_in, wqkv_ref[...]).astype(jnp.bfloat16).reshape(cols, total, 3 * channels)

        def pixel(p, inner):
            q = qkv[p, :, 0:channels]
            key = qkv[p, :, channels:2 * channels]
            value = qkv[p, :, 2 * channels:]
            spread = jnp.concatenate(
                [jnp.where(lane_head == i, q, jnp.zeros_like(q)) for i in range(HEADS)], axis=0
            )
            scores = lax.dot_general(
                key, spread, (((1,), (1,)), ((), ())), preferred_element_type=jnp.float32
            )
            top = jnp.max(scores, axis=0, keepdims=True)
            parts = jnp.exp2((scores - top) * factor)
            weights = (parts / jnp.sum(parts, axis=0, keepdims=True)).astype(jnp.bfloat16)
            mixed = lax.dot_general(
                weights, value, (((0,), (0,)), ((), ())), preferred_element_type=jnp.float32
            )
            result = jnp.zeros((total, channels), jnp.float32)
            for i in range(HEADS):
                result = jnp.where(lane_head == i, mixed[i * total:(i + 1) * total], result)
            ctx[p] = result.astype(jnp.bfloat16)
            return inner

        lax.fori_loop(0, cols, pixel, 0)
        done = normed_buf[...].astype(jnp.float32).reshape(cols * total, channels)
        done = done + dot(ctx[...].reshape(cols * total, channels), wout_ref[...])
        done = done.astype(jnp.bfloat16).reshape(cols, total, channels)
        for i in range(nt):
            stage[i, s] = done[:, i * frames:(i + 1) * frames].reshape(unit, channels)
        for k in range(1, nt):
            back(k, s).start()
        out_ref[t, s] = stage[t, s]
        return carry

    lax.fori_loop(0, span, attend_unit, 0)

    def drain(s, carry):
        for k in range(1, nt):
            back(k, s).wait_recv()
            back(k, s).wait_send()
            forward(k, s).wait_send()
        return carry

    lax.fori_loop(0, span, drain, 0)
    for index, (dr, dc) in enumerate(STEPS):
        @pl.when(jnp.logical_and(inside(h + dr, nh), inside(w + dc, nw)))
        def _(index=index):
            halo(index, 1).wait_send()
    for side, step in ((0, -1), (1, 1)):
        @pl.when(inside(t + step, nt))
        def _(side=side):
            edge(side, 1).wait_send()


def per_device(sizes, video, w_space, w_time, norm_gain, norm_bias, w_qkv, w_out):
    frames, rows, cols, channels = video.shape
    nt, nh, nw = sizes
    span = rows // nt
    unit = cols * frames
    total = nt * frames
    x = jnp.transpose(video, (1, 2, 0, 3))
    vmem = pl.BlockSpec(memory_space=pltpu.VMEM)
    bf16, f32, dma = jnp.bfloat16, jnp.float32, pltpu.SemaphoreType.DMA
    block = 2 if rows % 2 == 0 else 1
    pixels = rows * cols * frames
    lanes = math.gcd(channels, 128)
    out = pl.pallas_call(
        functools.partial(kernel, sizes),
        out_shape=jax.ShapeDtypeStruct((nt, span, unit, channels), bf16),
        in_specs=[pl.BlockSpec(memory_space=pl.ANY)] + [vmem] * 6,
        out_specs=vmem,
        scratch_shapes=[
            pltpu.VMEM((rows + 2, cols + 2, frames, channels), bf16),
            pltpu.VMEM((rows, unit, channels), bf16),
            pltpu.VMEM((2, rows, cols, channels), bf16),
            pltpu.VMEM((2, rows, cols, channels), bf16),
            pltpu.VMEM((channels // lanes, block * unit, lanes), f32),
            pltpu.VMEM((nt, span, unit, channels), bf16),
            pltpu.VMEM((nt, span, unit, channels), bf16),
            pltpu.VMEM((nt, span, unit, channels), bf16),
            pltpu.VMEM((cols, total, 3 * channels), bf16),
            pltpu.VMEM((cols, total, channels), bf16),
            pltpu.VMEM((cols, total, channels), bf16),
            pltpu.VMEM((8, channels), f32),
            pltpu.VMEM((nt, 8, channels), f32),
            pltpu.VMEM((nh, 8, channels), f32),
            pltpu.VMEM((nw, 8, channels), f32),
            dma, dma((len(STEPS),)), dma((len(STEPS),)), dma((2,)), dma((2,)),
            dma((nt, span)), dma((nt, span)), dma((nt, span)), dma((nt, span)),
            dma((nt,)), dma((nt,)), dma((nh,)), dma((nh,)), dma((nw,)), dma((nw,)),
        ],
        compiler_params=pltpu.CompilerParams(
            collective_id=0, has_side_effects=True, vmem_limit_bytes=52 * 1024 * 1024
        ),
        cost_estimate=pl.CostEstimate(
            flops=2 * pixels * channels * channels * 20,
            bytes_accessed=4 * pixels * channels, transcendentals=pixels * 64 * HEADS,
        ),
    )(
        x, w_space, w_time, norm_gain.reshape(1, channels), norm_bias.reshape(1, channels), w_qkv, w_out
    )
    return jnp.transpose(out.reshape(rows, cols, frames, channels), (2, 0, 1, 3))


def solution(mesh):
    sizes = tuple(mesh.shape[name] for name in ("tm", "height", "width"))
    placed = (P("tm", "height", "width", None), P(), P(), P(), P(), P(), P())
    return jax.shard_map(
        functools.partial(per_device, sizes),
        mesh=mesh,
        in_specs=placed,
        out_specs=P("tm", "height", "width", None),
        check_vma=False,
    )
```

time: 268 us -> 113 us (0.42)
  Pallas kernels: 0 us -> 105 us
  blocking collectives: 95.1 us -> 0 us
  local copies, waits for them, and re-layouts: 76.4 us -> 7.8 us
  matrix products: 38.9 us -> 0 us
  other arithmetic: 30.8 us -> 0 us
  starting transfers between devices: 16.6 us -> 0 us
  waiting for transfers between devices: 8.35 us -> 0 us
    pallas_call x0 -> x1, Pallas kernels: none -> 105 us  [per_device(): pl.pallas_call(functools.partial(kernel, sizes), out_shape=jax.ShapeDtype...]
    all_to_all x2 -> x0, blocking collectives: 53 us -> none  [the longest x1 28.2 us: per_device(): lax.all_to_all(slotted, 'tm', split_axis=1, concat_axis=0, tiled=True)]
    psum x1 -> x0, blocking collectives: 42.1 us -> none  [per_device(): lax.psum((local_sum, jnp.sum(grouped * grouped, axis=(0, 2))), ('tm', 'he...]
    dot_general x16 -> x0, matrix products: 38.9 us -> none  [the longest x1 11.6 us: attend(): jnp.einsum('fphd,gphd->phfg', projected[:, :, 0], projected[:, :, 1], pre...]
    reshape x2 -> x1, local copies, waits for them, and re-layouts: 24.6 us -> 3.62 us  [per_device(): out.reshape(rows, cols, frames, channels)]
    sub x1 -> x0, other arithmetic: 18.4 us -> none  [attend(): weights = jax.nn.softmax(scores, axis=-1).astype(jnp.bfloat16)]
    unnamed x20 -> x11, local copies, waits for them, and re-layouts: 22.5 us -> 4.18 us
    ppermute x6 -> x0, starting transfers between devices: 16.6 us -> none  [the longest x3 12.7 us: padded_2(): before = lax.ppermute(last, axis, up)]
  transfers between devices with their start and end apart: 6 -> 0, of which waited for: 5 -> 0; matrix products, arithmetic and copies ran while one was open for 0% -> 0% of each run, Pallas kernels for 0% -> 0%
where the time goes in v1:
time: 113 us
  Pallas kernels  105 us (93%)
  local copies, waits for them, and re-layouts  7.8 us (7%)
    pallas_call x1, Pallas kernels, per_device(): pl.pallas_call(functools.partial(kernel, sizes), out_shape=jax.ShapeDtype...  105 us
    unnamed x11, local copies, waits for them, and re-layouts  4.18 us
    reshape x1, local copies, waits for them, and re-layouts, per_device(): out.reshape(rows, cols, frames, channels)  3.62 us

profile of v1, /device:TPU:0, one launch (start us, length us, event | category | flops | bytes accessed | tf_op | source)
XLA Modules:
  0.0 112.6 jit_solution(2709097948773230400)
XLA Ops:
  0.0 0.0 copy-start
  0.0 0.0 copy-start.1
  0.0 0.0 copy-start.2
  0.0 0.0 copy-start.3
  0.0 0.0 copy-start.4
  0.0 4.2 %copy.13 = bf16[16,16,16,256]{3,0,2,1:T(8,128)(2,1)} copy(bf16[16,16,16,256]{3,2,1,0:T(8,128)(2,1)} %param.7) | data formatting | bytes 4194304 | tf_op args[0]
  4.2 0.0 copy-done
  4.2 0.0 copy-done.1
  4.2 0.0 copy-done.2
  4.2 0.0 copy-done.3
  4.2 0.0 copy-done.4
  4.2 104.7 %shard_map.73 = bf16[4,4,256,256]{3,2,1,0:T(8,128)(2,1)} custom-call(bf16[16,16,16,256]{3,2,1,0:T(8,128)(2,1)} %bitcast.12, bf16[3,3,256,256]{3,2,1,0:T(8,128)(2,1)} %wsp_ref.1, bf16[3,256,256]{2,1,0:T(8,128)(2,1)S(1)} %copy-done, f32[1,256]{1,0:T(1,128)S(1)} %bitcast.9, f32[1,256]{1,0:T(1,128)S(1)} %bitcast.10, bf16[256,768]{1,0:T(8,128)(2,1)S(1)} %copy-done.1, ...), custom_call_target="tpu_custom_call" | custom-call | flops 10737418240 | bytes 4194304 | tf_op jit(solution)/shard_map/pallas_call | solution.py:302
  108.9 3.6 %copy.12 = bf16[16,16,16,256]{3,1,0,2:T(8,128)(2,1)} copy(bf16[16,16,16,256]{3,2,1,0:T(8,128)(2,1)} %bitcast.11) | data formatting | bytes 4194304 | tf_op jit(solution)/shard_map/reshape | solution.py:337
Async XLA Ops:
  0.0 4.2 %copy-start = (bf16[3,256,256]{2,1,0:T(8,128)(2,1)S(1)}, bf16[3,256,256]{2,1,0:T(8,128)(2,1)}, u32[]{:S(2)}) copy-start(bf16[3,256,256]{2,1,0:T(8,128)(2,1)} %wt_ref.1) | copy-start | bytes 1179652
  0.0 4.2 %copy-start.1 = (bf16[256,768]{1,0:T(8,128)(2,1)S(1)}, bf16[256,768]{1,0:T(8,128)(2,1)}, u32[]{:S(2)}) copy-start(bf16[256,768]{1,0:T(8,128)(2,1)} %wqkv_ref.1) | copy-start | bytes 1179652
  0.0 4.2 %copy-start.2 = (bf16[256,256]{1,0:T(8,128)(2,1)S(1)}, bf16[256,256]{1,0:T(8,128)(2,1)}, u32[]{:S(2)}) copy-start(bf16[256,256]{1,0:T(8,128)(2,1)} %wout_ref.1) | copy-start | bytes 393220
  0.0 4.2 %copy-start.3 = (f32[256]{0:T(256)S(1)}, f32[256]{0:T(256)}, u32[]{:S(2)}) copy-start(f32[256]{0:T(256)} %param.10) | copy-start | bytes 3076
  0.0 4.2 %copy-start.4 = (f32[256]{0:T(256)S(1)}, f32[256]{0:T(256)}, u32[]{:S(2)}) copy-start(f32[256]{0:T(256)} %param.11) | copy-start | bytes 3076

commit v2 on v1

--- a/solution.py
+++ b/solution.py
@@ -214,6 +214,20 @@
     bias = bias_ref[...]
 
     lane_head = lax.broadcasted_iota(jnp.int32, (total, channels), 1) // head
+    within = 2 if HEADS % 2 == 0 else 1
+    pairs = HEADS // within
+    together = math.gcd(cols, 4)
+
+    def split_pairs(v):
+        return jnp.concatenate(
+            [jnp.where(lane_head // within == i, v, jnp.zeros_like(v)) for i in range(pairs)], axis=0
+        )
+
+    def split_within(v):
+        return jnp.concatenate(
+            [jnp.where(lane_head % within == i, v, jnp.zeros_like(v)) for i in range(within)], axis=0
+        )
+
     factor = math.log2(math.e) / math.sqrt(head)
 
     def back(k, s):
@@ -234,29 +248,34 @@
         rows_in = normed_buf[...].reshape(cols * total, channels)
         qkv[...] = dot(rows_in, wqkv_ref[...]).astype(jnp.bfloat16).reshape(cols, total, 3 * channels)
 
-        def pixel(p, inner):
-            q = qkv[p, :, 0:channels]
-            key = qkv[p, :, channels:2 * channels]
-            value = qkv[p, :, 2 * channels:]
-            spread = jnp.concatenate(
-                [jnp.where(lane_head == i, q, jnp.zeros_like(q)) for i in range(HEADS)], axis=0
-            )
-            scores = lax.dot_general(
-                key, spread, (((1,), (1,)), ((), ())), preferred_element_type=jnp.float32
-            )
-            top = jnp.max(scores, axis=0, keepdims=True)
-            parts = jnp.exp2((scores - top) * factor)
-            weights = (parts / jnp.sum(parts, axis=0, keepdims=True)).astype(jnp.bfloat16)
-            mixed = lax.dot_general(
-                weights, value, (((0,), (0,)), ((), ())), preferred_element_type=jnp.float32
-            )
-            result = jnp.zeros((total, channels), jnp.float32)
-            for i in range(HEADS):
-                result = jnp.where(lane_head == i, mixed[i * total:(i + 1) * total], result)
-            ctx[p] = result.astype(jnp.bfloat16)
+        def pixel_group(g, inner):
+            ps = [g * together + i for i in range(together)]
+            scores = []
+            for p in ps:
+                q = qkv[p, :, 0:channels]
+                key = qkv[p, :, channels:2 * channels]
+                scores.append(lax.dot_general(
+                    split_pairs(key), split_within(q), (((1,), (1,)), ((), ())),
+                    preferred_element_type=jnp.float32,
+                ).reshape(pairs, total, within * total))
+            weights = []
+            for value in scores:
+                top = jnp.max(value, axis=1, keepdims=True)
+                parts = jnp.exp2((value - top) * factor)
+                share = 1.0 / jnp.sum(parts, axis=1, keepdims=True)
+                weights.append((parts * share).astype(jnp.bfloat16).reshape(pairs * total, within * total))
+            for p, value in zip(ps, weights):
+                mixed = lax.dot_general(
+                    value, split_pairs(qkv[p, :, 2 * channels:]), (((0,), (0,)), ((), ())),
+                    preferred_element_type=jnp.float32,
+                )
+                result = mixed[0:total]
+                for i in range(1, within):
+                    result = jnp.where(lane_head % within == i, mixed[i * total:(i + 1) * total], result)
+                ctx[p] = result.astype(jnp.bfloat16)
             return inner
 
-        lax.fori_loop(0, cols, pixel, 0)
+        lax.fori_loop(0, cols // together, pixel_group, 0)
         done = normed_buf[...].astype(jnp.float32).reshape(cols * total, channels)
         done = done + dot(ctx[...].reshape(cols * total, channels), wout_ref[...])
         done = done.astype(jnp.bfloat16).reshape(cols, total, channels)

time: 113 us -> 93.9 us (0.83)
  Pallas kernels: 105 us -> 85.8 us
    pallas_call x1, Pallas kernels: 105 us -> 85.8 us  [per_device(): pl.pallas_call(functools.partial(kernel, sizes), out_shape=jax.ShapeDtype...]
where the time goes in v2:
time: 93.9 us; the launch traced here: 93.6 us
  Pallas kernels  85.8 us (91%)
  local copies, waits for them, and re-layouts  7.8 us (8%)
    pallas_call x1, Pallas kernels, per_device(): pl.pallas_call(functools.partial(kernel, sizes), out_shape=jax.ShapeDtype...  85.8 us
    unnamed x11, local copies, waits for them, and re-layouts  4.18 us
    reshape x1, local copies, waits for them, and re-layouts, per_device(): out.reshape(rows, cols, frames, channels)  3.62 us

profile of v2, /device:TPU:0, one launch (start us, length us, event | category | flops | bytes accessed | tf_op | source)
XLA Modules:
  0.0 93.6 jit_solution(6408252529846286602)
XLA Ops:
  0.0 0.0 copy-start
  0.0 0.0 copy-start.1
  0.0 0.0 copy-start.2
  0.0 0.0 copy-start.3
  0.0 0.0 copy-start.4
  0.0 4.2 %copy.13 = bf16[16,16,16,256]{3,0,2,1:T(8,128)(2,1)} copy(bf16[16,16,16,256]{3,2,1,0:T(8,128)(2,1)} %param.7) | data formatting | bytes 4194304 | tf_op args[0]
  4.2 0.0 copy-done
  4.2 0.0 copy-done.1
  4.2 0.0 copy-done.2
  4.2 0.0 copy-done.3
  4.2 0.0 copy-done.4
  4.2 85.8 %shard_map.73 = bf16[4,4,256,256]{3,2,1,0:T(8,128)(2,1)} custom-call(bf16[16,16,16,256]{3,2,1,0:T(8,128)(2,1)} %bitcast.12, bf16[3,3,256,256]{3,2,1,0:T(8,128)(2,1)} %wsp_ref.1, bf16[3,256,256]{2,1,0:T(8,128)(2,1)S(1)} %copy-done, f32[1,256]{1,0:T(1,128)S(1)} %bitcast.9, f32[1,256]{1,0:T(1,128)S(1)} %bitcast.10, bf16[256,768]{1,0:T(8,128)(2,1)S(1)} %copy-done.1, ...), custom_call_target="tpu_custom_call" | custom-call | flops 10737418240 | bytes 4194304 | tf_op jit(solution)/shard_map/pallas_call | solution.py:321
  90.0 3.6 %copy.12 = bf16[16,16,16,256]{3,1,0,2:T(8,128)(2,1)} copy(bf16[16,16,16,256]{3,2,1,0:T(8,128)(2,1)} %bitcast.11) | data formatting | bytes 4194304 | tf_op jit(solution)/shard_map/reshape | solution.py:356
Async XLA Ops:
  0.0 4.2 %copy-start = (bf16[3,256,256]{2,1,0:T(8,128)(2,1)S(1)}, bf16[3,256,256]{2,1,0:T(8,128)(2,1)}, u32[]{:S(2)}) copy-start(bf16[3,256,256]{2,1,0:T(8,128)(2,1)} %wt_ref.1) | copy-start | bytes 1179652
  0.0 4.2 %copy-start.1 = (bf16[256,768]{1,0:T(8,128)(2,1)S(1)}, bf16[256,768]{1,0:T(8,128)(2,1)}, u32[]{:S(2)}) copy-start(bf16[256,768]{1,0:T(8,128)(2,1)} %wqkv_ref.1) | copy-start | bytes 1179652
  0.0 4.2 %copy-start.2 = (bf16[256,256]{1,0:T(8,128)(2,1)S(1)}, bf16[256,256]{1,0:T(8,128)(2,1)}, u32[]{:S(2)}) copy-start(bf16[256,256]{1,0:T(8,128)(2,1)} %wout_ref.1) | copy-start | bytes 393220
  0.0 4.2 %copy-start.3 = (f32[256]{0:T(256)S(1)}, f32[256]{0:T(256)}, u32[]{:S(2)}) copy-start(f32[256]{0:T(256)} %param.10) | copy-start | bytes 3076
  0.0 4.2 %copy-start.4 = (f32[256]{0:T(256)S(1)}, f32[256]{0:T(256)}, u32[]{:S(2)}) copy-start(f32[256]{0:T(256)} %param.11) | copy-start | bytes 3076

commit v3 on v2

--- a/solution.py
+++ b/solution.py
@@ -25,13 +25,13 @@
 
 def kernel(
     sizes, x_ref, wsp_ref, wt_ref, gain_ref, bias_ref, wqkv_ref, wout_ref, out_ref,
-    pad, spat, edge_out, edge_in, tmp, piece, recv, stage, qkv, ctx, normed_buf,
+    pad, spat, edge_out, edge_in, tmp, turn, turn_out, piece, recv, stage, qkv, ctx, normed_buf,
     stat, ex_t, ex_h, ex_w,
-    load_sem, halo_send, halo_recv, edge_send, edge_recv, fwd_send, fwd_recv,
+    halo_send, halo_recv, edge_send, edge_recv, fwd_send, fwd_recv,
     back_send, back_recv, t_send, t_recv, h_send, h_recv, w_send, w_recv,
 ):
     nt, nh, nw = sizes
-    rows, cols, frames, channels = x_ref.shape
+    frames, rows, cols, channels = x_ref.shape
     span = rows // nt
     unit = cols * frames
     total = nt * frames
@@ -55,12 +55,28 @@
     for k in range(1, nw):
         pl.semaphore_signal(barrier, inc=1, device_id=(t, h, lax.rem(w + k, nw)), device_id_type=MESH)
 
-    load = pltpu.make_async_copy(x_ref, pad.at[pl.ds(1, rows), pl.ds(1, cols)], load_sem)
-    load.start()
+    lanes = tmp.shape[2]
+    halves = channels // lanes
+    two = 2 if rows % 2 == 0 else 1
+
+    def turn_in(step, carry):
+        for b in range(two):
+            r = step * two + b
+            for c in range(halves):
+                turn[b * halves + c] = x_ref[:, r, :, c * lanes:(c + 1) * lanes].astype(
+                    jnp.float32
+                ).reshape(unit, lanes)
+            for i in range(cols):
+                pad[r + 1, i + 1] = jnp.concatenate(
+                    [turn[b * halves + c, pl.ds(i, frames, stride=cols), :] for c in range(halves)], axis=1
+                ).astype(jnp.bfloat16)
+        return carry
+
+    lax.fori_loop(0, rows // two, turn_in, 0)
     pl.semaphore_wait(barrier, count + (nt - 1) + (nh - 1) + (nw - 1))
 
     def span_of(step, size):
-        src = {-1: pl.ds(0, 1), 0: pl.ds(0, size), 1: pl.ds(size - 1, 1)}[step]
+        src = {-1: pl.ds(1, 1), 0: pl.ds(1, size), 1: pl.ds(size, 1)}[step]
         dst = {-1: pl.ds(size + 1, 1), 0: pl.ds(1, size), 1: pl.ds(0, 1)}[step]
         return src, dst
 
@@ -68,7 +84,7 @@
         dr, dc = STEPS[index]
         (src_r, dst_r), (src_c, dst_c) = span_of(dr, rows), span_of(dc, cols)
         return pltpu.make_async_remote_copy(
-            src_ref=x_ref.at[src_r, src_c], dst_ref=pad.at[dst_r, dst_c],
+            src_ref=pad.at[src_r, src_c], dst_ref=pad.at[dst_r, dst_c],
             send_sem=halo_send.at[index], recv_sem=halo_recv.at[index],
             device_id=(t, h + sign * dr, w + sign * dc), device_id_type=MESH,
         )
@@ -82,56 +98,52 @@
         def _(dr=dr, dc=dc):
             dst_r, dst_c = span_of(dr, rows)[1], span_of(dc, cols)[1]
             pad[dst_r, dst_c] = jnp.zeros((dst_r.size, dst_c.size, frames, channels), pad.dtype)
-    load.wait()
     for index, (dr, dc) in enumerate(STEPS):
         @pl.when(jnp.logical_and(inside(h - dr, nh), inside(w - dc, nw)))
         def _(index=index):
             halo(index, -1).wait_recv()
 
-    block = 2 if rows % 2 == 0 else 1
-
-    def conv_step(step, carry):
-        r = step * block
-        acc = jnp.zeros((block * unit, channels), jnp.float32)
-        for i in range(3):
-            for j in range(3):
-                taps = pad[pl.ds(r + i, block), pl.ds(j, cols)].reshape(block * unit, channels)
-                acc = acc + dot(taps, wsp_ref[i, j])
-        value = acc.astype(jnp.bfloat16)
-        spat[pl.ds(r, block)] = value.reshape(block, unit, channels)
-        lanes = tmp.shape[2]
-        for c in range(channels // lanes):
-            tmp[c] = value[:, c * lanes:(c + 1) * lanes].astype(jnp.float32)
-        for b in range(block):
-            for side, frame in ((0, 0), (1, frames - 1)):
-                edge_out[side, r + b] = jnp.concatenate(
-                    [tmp[c, pl.ds(b * unit + frame, cols, stride=frames), :]
-                     for c in range(channels // lanes)], axis=1
-                ).astype(jnp.bfloat16)
-        return carry
-
-    lax.fori_loop(0, rows // block, conv_step, 0)
-
-    def edge(side, sign):
+    block = 2 if nt % 2 == 0 else 1
+
+    def edge(side, s, sign):
         step = (-1, 1)[side]
         return pltpu.make_async_remote_copy(
-            src_ref=edge_out.at[side], dst_ref=edge_in.at[side],
-            send_sem=edge_send.at[side], recv_sem=edge_recv.at[side],
+            src_ref=edge_out.at[side, s], dst_ref=edge_in.at[side, s],
+            send_sem=edge_send.at[side, s], recv_sem=edge_recv.at[side, s],
             device_id=(t + sign * step, h, w), device_id_type=MESH,
         )
 
+    def conv_round(s):
+        for first in range(0, nt, block):
+            acc = jnp.zeros((block * unit, channels), jnp.float32)
+            for i in range(3):
+                for j in range(3):
+                    taps = jnp.concatenate(
+                        [pad[(first + b) * span + s + i, pl.ds(j, cols)].reshape(unit, channels)
+                         for b in range(block)], axis=0
+                    )
+                    acc = acc + dot(taps, wsp_ref[i, j])
+            value = acc.astype(jnp.bfloat16)
+            for b in range(block):
+                k = first + b
+                here = value[b * unit:(b + 1) * unit]
+                spat[k * span + s] = here
+                for c in range(halves):
+                    tmp[k * halves + c] = here[:, c * lanes:(c + 1) * lanes].astype(jnp.float32)
+                for side, frame in ((0, 0), (1, frames - 1)):
+                    edge_out[side, s, k] = jnp.concatenate(
+                        [tmp[k * halves + c, pl.ds(frame, cols, stride=frames), :] for c in range(halves)],
+                        axis=1,
+                    ).astype(jnp.bfloat16)
+        for side, step in ((0, -1), (1, 1)):
+            @pl.when(inside(t + step, nt))
+            def _(side=side):
+                edge(side, s, 1).start()
+
     for side, step in ((0, -1), (1, 1)):
-        @pl.when(inside(t + step, nt))
-        def _(side=side):
-            edge(side, 1).start()
-
         @pl.when(jnp.logical_not(inside(t - step, nt)))
         def _(side=side):
             edge_in[side] = jnp.zeros(edge_in.shape[1:], edge_in.dtype)
-    for side, step in ((0, -1), (1, 1)):
-        @pl.when(inside(t - step, nt))
-        def _(side=side):
-            edge(side, -1).wait_recv()
 
     stat[...] = jnp.zeros_like(stat)
     frame_of = lax.rem(lax.broadcasted_iota(jnp.int32, (unit, channels), 0), frames)
@@ -144,15 +156,21 @@
             device_id=(to, h, w), device_id_type=MESH,
         )
 
-    def time_step(s, carry):
+    def spread(v):
+        return jnp.broadcast_to(v[:, None, :], (cols, frames, channels)).reshape(unit, channels)
+
+    def time_round(s):
+        for side, step in ((0, -1), (1, 1)):
+            @pl.when(inside(t - step, nt))
+            def _(side=side):
+                edge(side, s, -1).wait_recv()
         for k in list(range(1, nt)) + [0]:
-            r = lax.rem(t + k, nt) * span + s
-            here = spat[r]
+            chunk = lax.rem(t + k, nt)
+            here = spat[chunk * span + s]
             before = pltpu.roll(dot(here, wt_ref[0]), 1, 0)
             after = pltpu.roll(dot(here, wt_ref[2]), unit - 1, 0)
-            spread = lambda v: jnp.broadcast_to(v[:, None, :], (cols, frames, channels)).reshape(unit, channels)
-            first = spread(dot(edge_in[1, r], wt_ref[0]))
-            last = spread(dot(edge_in[0, r], wt_ref[2]))
+            first = spread(dot(edge_in[1, s, chunk], wt_ref[0]))
+            last = spread(dot(edge_in[0, s, chunk], wt_ref[2]))
             value = here.astype(jnp.float32) + dot(here, wt_ref[1])
             value = value + jnp.where(frame_of == 0, first, before)
             value = value + jnp.where(frame_of == frames - 1, last, after)
@@ -165,9 +183,15 @@
             wide = value.astype(jnp.float32)
             stat[0:1] += jnp.sum(wide, axis=0, keepdims=True)
             stat[1:2] += jnp.sum(wide * wide, axis=0, keepdims=True)
+
+    def both(s, carry):
+        conv_round(s)
+        time_round(s - 1)
         return carry
 
-    lax.fori_loop(0, span, time_step, 0)
+    conv_round(0)
+    lax.fori_loop(1, span, both, 0)
+    time_round(span - 1)
 
     def exchange(slots, size, me, device, send, arrive):
         slots[me] = stat[...]
@@ -233,7 +257,7 @@
     def back(k, s):
         to = lax.rem(t + k, nt)
         return pltpu.make_async_remote_copy(
-            src_ref=stage.at[to, s], dst_ref=out_ref.at[t, s],
+            src_ref=stage.at[to, s], dst_ref=out_ref.at[:, t * span + s],
             send_sem=back_send.at[k, s], recv_sem=back_recv.at[k, s],
             device_id=(to, h, w), device_id_type=MESH,
         )
@@ -278,12 +302,17 @@
         lax.fori_loop(0, cols // together, pixel_group, 0)
         done = normed_buf[...].astype(jnp.float32).reshape(cols * total, channels)
         done = done + dot(ctx[...].reshape(cols * total, channels), wout_ref[...])
-        done = done.astype(jnp.bfloat16).reshape(cols, total, channels)
+        for c in range(halves):
+            turn_out[c] = done[:, c * lanes:(c + 1) * lanes]
         for i in range(nt):
-            stage[i, s] = done[:, i * frames:(i + 1) * frames].reshape(unit, channels)
+            for f in range(frames):
+                stage[i, s, f] = jnp.concatenate(
+                    [turn_out[c, pl.ds(i * frames + f, cols, stride=total), :] for c in range(halves)],
+                    axis=1,
+                ).astype(jnp.bfloat16)
         for k in range(1, nt):
             back(k, s).start()
-        out_ref[t, s] = stage[t, s]
+        out_ref[:, t * span + s] = stage[t, s]
         return carry
 
     lax.fori_loop(0, span, attend_unit, 0)
@@ -303,7 +332,8 @@
     for side, step in ((0, -1), (1, 1)):
         @pl.when(inside(t + step, nt))
         def _(side=side):
-            edge(side, 1).wait_send()
+            for s in range(span):
+                edge(side, s, 1).wait_send()
 
 
 def per_device(sizes, video, w_space, w_time, norm_gain, norm_bias, w_qkv, w_out):
@@ -312,26 +342,28 @@
     span = rows // nt
     unit = cols * frames
     total = nt * frames
-    x = jnp.transpose(video, (1, 2, 0, 3))
     vmem = pl.BlockSpec(memory_space=pltpu.VMEM)
     bf16, f32, dma = jnp.bfloat16, jnp.float32, pltpu.SemaphoreType.DMA
-    block = 2 if rows % 2 == 0 else 1
+    two = 2 if rows % 2 == 0 else 1
     pixels = rows * cols * frames
     lanes = math.gcd(channels, 128)
+    halves = channels // lanes
     out = pl.pallas_call(
         functools.partial(kernel, sizes),
-        out_shape=jax.ShapeDtypeStruct((nt, span, unit, channels), bf16),
-        in_specs=[pl.BlockSpec(memory_space=pl.ANY)] + [vmem] * 6,
+        out_shape=jax.ShapeDtypeStruct(video.shape, bf16),
+        in_specs=[vmem] * 7,
         out_specs=vmem,
         scratch_shapes=[
             pltpu.VMEM((rows + 2, cols + 2, frames, channels), bf16),
             pltpu.VMEM((rows, unit, channels), bf16),
-            pltpu.VMEM((2, rows, cols, channels), bf16),
-            pltpu.VMEM((2, rows, cols, channels), bf16),
-            pltpu.VMEM((channels // lanes, block * unit, lanes), f32),
+            pltpu.VMEM((2, span, nt, cols, channels), bf16),
+            pltpu.VMEM((2, span, nt, cols, channels), bf16),
+            pltpu.VMEM((nt * halves, unit, lanes), f32),
+            pltpu.VMEM((two * halves, unit, lanes), f32),
+            pltpu.VMEM((halves, cols * total, lanes), f32),
             pltpu.VMEM((nt, span, unit, channels), bf16),
             pltpu.VMEM((nt, span, unit, channels), bf16),
-            pltpu.VMEM((nt, span, unit, channels), bf16),
+            pltpu.VMEM((nt, span, frames, cols, channels), bf16),
             pltpu.VMEM((cols, total, 3 * channels), bf16),
             pltpu.VMEM((cols, total, channels), bf16),
             pltpu.VMEM((cols, total, channels), bf16),
@@ -339,7 +371,7 @@
             pltpu.VMEM((nt, 8, channels), f32),
             pltpu.VMEM((nh, 8, channels), f32),
             pltpu.VMEM((nw, 8, channels), f32),
-            dma, dma((len(STEPS),)), dma((len(STEPS),)), dma((2,)), dma((2,)),
+            dma((len(STEPS),)), dma((len(STEPS),)), dma((2, span)), dma((2, span)),
             dma((nt, span)), dma((nt, span)), dma((nt, span)), dma((nt, span)),
             dma((nt,)), dma((nt,)), dma((nh,)), dma((nh,)), dma((nw,)), dma((nw,)),
         ],
@@ -351,9 +383,9 @@
             bytes_accessed=4 * pixels * channels, transcendentals=pixels * 64 * HEADS,
         ),
     )(
-        x, w_space, w_time, norm_gain.reshape(1, channels), norm_bias.reshape(1, channels), w_qkv, w_out
+        video, w_space, w_time, norm_gain.reshape(1, channels), norm_bias.reshape(1, channels), w_qkv, w_out
     )
-    return jnp.transpose(out.reshape(rows, cols, frames, channels), (2, 0, 1, 3))
+    return out
 
 
 def solution(mesh):

time: 93.9 us -> 88.2 us (0.939)
  Pallas kernels: 85.8 us -> 80.5 us
    pallas_call x1, Pallas kernels: 85.8 us -> 80.5 us  [per_device(): pl.pallas_call(functools.partial(kernel, sizes), out_shape=jax.ShapeDtype...]
    reshape x1 -> x0, local copies, waits for them, and re-layouts: 3.62 us -> none  [per_device(): out.reshape(rows, cols, frames, channels)]
    unnamed x11, local copies, waits for them, and re-layouts: 4.18 us -> 7.35 us
where the time goes in v3:
time: 88.2 us; the launch traced here: 87.9 us
  Pallas kernels  80.5 us (91%)
  local copies, waits for them, and re-layouts  7.35 us (8%)
    pallas_call x1, Pallas kernels, per_device(): pl.pallas_call(functools.partial(kernel, sizes), out_shape=jax.ShapeDtype...  80.5 us
    unnamed x11, local copies, waits for them, and re-layouts  7.35 us

profile of v3, /device:TPU:0, one launch (start us, length us, event | category | flops | bytes accessed | tf_op | source)
XLA Modules:
  0.0 87.9 jit_solution(5655598418185743253)
XLA Ops:
  0.0 0.0 copy-start
  0.0 1.0 %copy-done = bf16[3,256,256]{2,1,0:T(8,128)(2,1)S(1)} copy-done((bf16[3,256,256]{2,1,0:T(8,128)(2,1)S(1)}, bf16[3,256,256]{2,1,0:T(8,128)(2,1)}, u32[]{:S(2)}) %copy-start) | copy-done | bytes 393240
  1.0 0.0 copy-start.1
  1.0 1.0 %copy-done.1 = bf16[256,768]{1,0:T(8,128)(2,1)S(1)} copy-done((bf16[256,768]{1,0:T(8,128)(2,1)S(1)}, bf16[256,768]{1,0:T(8,128)(2,1)}, u32[]{:S(2)}) %copy-start.1) | copy-done | bytes 393240
  2.0 0.0 copy-start.2
  2.0 0.9 %copy-done.2 = bf16[256,256]{1,0:T(8,128)(2,1)S(1)} copy-done((bf16[256,256]{1,0:T(8,128)(2,1)S(1)}, bf16[256,256]{1,0:T(8,128)(2,1)}, u32[]{:S(2)}) %copy-start.2) | copy-done | bytes 131096
  2.9 0.0 copy-start.3
  2.9 0.7 copy-done.3
  3.6 0.0 copy-start.4
  3.6 0.7 copy-done.4
  4.3 80.5 %shard_map.73 = bf16[16,16,16,256]{3,2,1,0:T(8,128)(2,1)} custom-call(bf16[16,16,16,256]{3,2,1,0:T(8,128)(2,1)} %x_ref.1, bf16[3,3,256,256]{3,2,1,0:T(8,128)(2,1)} %wsp_ref.1, bf16[3,256,256]{2,1,0:T(8,128)(2,1)S(1)} %copy-done, f32[1,256]{1,0:T(1,128)S(1)} %bitcast.2, f32[1,256]{1,0:T(1,128)S(1)} %bitcast.3, bf16[256,768]{1,0:T(8,128)(2,1)S(1)} %copy-done.1, ...), custom_call_target="tpu_custom_call" | custom-call | flops 10737418240 | bytes 4194304 | tf_op jit(solution)/shard_map/pallas_call | solution.py:351
  84.8 3.1 %copy.9 = bf16[16,16,16,256]{3,2,1,0:T(8,128)(2,1)} copy(bf16[16,16,16,256]{3,2,1,0:T(8,128)(2,1)} %shard_map.73) | data formatting | bytes 4194304
Async XLA Ops:
  0.0 1.0 %copy-start = (bf16[3,256,256]{2,1,0:T(8,128)(2,1)S(1)}, bf16[3,256,256]{2,1,0:T(8,128)(2,1)}, u32[]{:S(2)}) copy-start(bf16[3,256,256]{2,1,0:T(8,128)(2,1)} %wt_ref.1) | copy-start | bytes 1179652
  1.0 1.0 %copy-start.1 = (bf16[256,768]{1,0:T(8,128)(2,1)S(1)}, bf16[256,768]{1,0:T(8,128)(2,1)}, u32[]{:S(2)}) copy-start(bf16[256,768]{1,0:T(8,128)(2,1)} %wqkv_ref.1) | copy-start | bytes 1179652
  2.0 0.9 %copy-start.2 = (bf16[256,256]{1,0:T(8,128)(2,1)S(1)}, bf16[256,256]{1,0:T(8,128)(2,1)}, u32[]{:S(2)}) copy-start(bf16[256,256]{1,0:T(8,128)(2,1)} %wout_ref.1) | copy-start | bytes 393220
  2.9 0.7 copy-start.3
  3.6 0.7 copy-start.4

commit v4 on v3

--- a/solution.py
+++ b/solution.py
@@ -24,10 +24,11 @@
 
 
 def kernel(
-    sizes, x_ref, wsp_ref, wt_ref, gain_ref, bias_ref, wqkv_ref, wout_ref, out_ref,
+    sizes, x_hbm, wsp_hbm, wt_hbm, gain_ref, bias_ref, wqkv_hbm, wout_hbm, out_ref,
+    x_ref, wsp_ref, wt_ref, wqkv_ref, wout_ref,
     pad, spat, edge_out, edge_in, tmp, turn, turn_out, piece, recv, stage, qkv, ctx, normed_buf,
     stat, ex_t, ex_h, ex_w,
-    halo_send, halo_recv, edge_send, edge_recv, fwd_send, fwd_recv,
+    load_sem, own_sem, halo_send, halo_recv, edge_send, edge_recv, fwd_send, fwd_recv,
     back_send, back_recv, t_send, t_recv, h_send, h_recv, w_send, w_recv,
 ):
     nt, nh, nw = sizes
@@ -54,6 +55,16 @@
         pl.semaphore_signal(barrier, inc=1, device_id=(t, lax.rem(h + k, nh), w), device_id_type=MESH)
     for k in range(1, nw):
         pl.semaphore_signal(barrier, inc=1, device_id=(t, h, lax.rem(w + k, nw)), device_id_type=MESH)
+
+    loads = [
+        pltpu.make_async_copy(src, dst, load_sem.at[i])
+        for i, (src, dst) in enumerate((
+            (x_hbm, x_ref), (wsp_hbm, wsp_ref), (wt_hbm, wt_ref), (wqkv_hbm, wqkv_ref), (wout_hbm, wout_ref),
+        ))
+    ]
+    for load in loads:
+        load.start()
+    loads[0].wait()
 
     lanes = tmp.shape[2]
     halves = channels // lanes
@@ -146,7 +157,7 @@
             edge_in[side] = jnp.zeros(edge_in.shape[1:], edge_in.dtype)
 
     stat[...] = jnp.zeros_like(stat)
-    frame_of = lax.rem(lax.broadcasted_iota(jnp.int32, (unit, channels), 0), frames)
+    frame_of = lax.rem(lax.broadcasted_iota(jnp.int32, (block * unit, channels), 0), frames)
 
     def forward(k, s):
         to = lax.rem(t + k, nt)
@@ -157,29 +168,32 @@
         )
 
     def spread(v):
-        return jnp.broadcast_to(v[:, None, :], (cols, frames, channels)).reshape(unit, channels)
+        return jnp.broadcast_to(v[:, None, :], (block * cols, frames, channels)).reshape(block * unit, channels)
 
     def time_round(s):
         for side, step in ((0, -1), (1, 1)):
             @pl.when(inside(t - step, nt))
             def _(side=side):
                 edge(side, s, -1).wait_recv()
-        for k in list(range(1, nt)) + [0]:
-            chunk = lax.rem(t + k, nt)
-            here = spat[chunk * span + s]
+        order = list(range(1, nt)) + [0]
+        for place in range(0, nt, block):
+            ks = order[place:place + block]
+            chunks = [lax.rem(t + k, nt) for k in ks]
+            here = jnp.concatenate([spat[chunk * span + s] for chunk in chunks], axis=0)
+            ends = [jnp.concatenate([edge_in[side, s, chunk] for chunk in chunks], axis=0) for side in (0, 1)]
+            value = here.astype(jnp.float32) + dot(here, wt_ref[1])
             before = pltpu.roll(dot(here, wt_ref[0]), 1, 0)
-            after = pltpu.roll(dot(here, wt_ref[2]), unit - 1, 0)
-            first = spread(dot(edge_in[1, s, chunk], wt_ref[0]))
-            last = spread(dot(edge_in[0, s, chunk], wt_ref[2]))
-            value = here.astype(jnp.float32) + dot(here, wt_ref[1])
-            value = value + jnp.where(frame_of == 0, first, before)
-            value = value + jnp.where(frame_of == frames - 1, last, after)
+            value = value + jnp.where(frame_of == 0, spread(dot(ends[1], wt_ref[0])), before)
+            after = pltpu.roll(dot(here, wt_ref[2]), block * unit - 1, 0)
+            value = value + jnp.where(frame_of == frames - 1, spread(dot(ends[0], wt_ref[2])), after)
             value = value.astype(jnp.bfloat16)
-            if k:
-                piece[k, s] = value
-                forward(k, s).start()
-            else:
-                recv[t, s] = value
+            for b, k in enumerate(ks):
+                part = value[b * unit:(b + 1) * unit]
+                if k:
+                    piece[k, s] = part
+                    forward(k, s).start()
+                else:
+                    recv[t, s] = part
             wide = value.astype(jnp.float32)
             stat[0:1] += jnp.sum(wide, axis=0, keepdims=True)
             stat[1:2] += jnp.sum(wide * wide, axis=0, keepdims=True)
@@ -189,6 +203,8 @@
         time_round(s - 1)
         return carry
 
+    for load in loads[1:]:
+        load.wait()
     conv_round(0)
     lax.fori_loop(1, span, both, 0)
     time_round(span - 1)
@@ -240,7 +256,7 @@
     lane_head = lax.broadcasted_iota(jnp.int32, (total, channels), 1) // head
     within = 2 if HEADS % 2 == 0 else 1
     pairs = HEADS // within
-    together = math.gcd(cols, 4)
+    together = math.gcd(cols, 8)
 
     def split_pairs(v):
         return jnp.concatenate(
@@ -261,6 +277,9 @@
             send_sem=back_send.at[k, s], recv_sem=back_recv.at[k, s],
             device_id=(to, h, w), device_id_type=MESH,
         )
+
+    def own(s):
+        return pltpu.make_async_copy(stage.at[t, s], out_ref.at[:, t * span + s], own_sem.at[s])
 
     def attend_unit(s, carry):
         for k in range(1, nt):
@@ -272,31 +291,37 @@
         rows_in = normed_buf[...].reshape(cols * total, channels)
         qkv[...] = dot(rows_in, wqkv_ref[...]).astype(jnp.bfloat16).reshape(cols, total, 3 * channels)
 
+        def scores_of(p):
+            return lax.dot_general(
+                split_pairs(qkv[p, :, channels:2 * channels]), split_within(qkv[p, :, 0:channels]),
+                (((1,), (1,)), ((), ())), preferred_element_type=jnp.float32,
+            ).reshape(pairs, total, within * total)
+
+        def weights_of(value):
+            top = jnp.max(value, axis=1, keepdims=True)
+            parts = jnp.exp2((value - top) * factor)
+            share = 1.0 / jnp.sum(parts, axis=1, keepdims=True)
+            return (parts * share).astype(jnp.bfloat16).reshape(pairs * total, within * total)
+
+        def mix(p, value):
+            mixed = lax.dot_general(
+                value, split_pairs(qkv[p, :, 2 * channels:]), (((0,), (0,)), ((), ())),
+                preferred_element_type=jnp.float32,
+            )
+            result = mixed[0:total]
+            for i in range(1, within):
+                result = jnp.where(lane_head % within == i, mixed[i * total:(i + 1) * total], result)
+            ctx[p] = result.astype(jnp.bfloat16)
+
         def pixel_group(g, inner):
-            ps = [g * together + i for i in range(together)]
-            scores = []
-            for p in ps:
-                q = qkv[p, :, 0:channels]
-                key = qkv[p, :, channels:2 * channels]
-                scores.append(lax.dot_general(
-                    split_pairs(key), split_within(q), (((1,), (1,)), ((), ())),
-                    preferred_element_type=jnp.float32,
-                ).reshape(pairs, total, within * total))
-            weights = []
-            for value in scores:
-                top = jnp.max(value, axis=1, keepdims=True)
-                parts = jnp.exp2((value - top) * factor)
-                share = 1.0 / jnp.sum(parts, axis=1, keepdims=True)
-                weights.append((parts * share).astype(jnp.bfloat16).reshape(pairs * total, within * total))
-            for p, value in zip(ps, weights):
-                mixed = lax.dot_general(
-                    value, split_pairs(qkv[p, :, 2 * channels:]), (((0,), (0,)), ((), ())),
-                    preferred_element_type=jnp.float32,
-                )
-                result = mixed[0:total]
-                for i in range(1, within):
-                    result = jnp.where(lane_head % within == i, mixed[i * total:(i + 1) * total], result)
-                ctx[p] = result.astype(jnp.bfloat16)
+            scores, weights = {}, {}
+            for step in range(together + 2):
+                if step < together:
+                    scores[step] = scores_of(g * together + step)
+                if 0 <= step - 1 < together:
+                    weights[step - 1] = weights_of(scores.pop(step - 1))
+                if 0 <= step - 2 < together:
+                    mix(g * together + step - 2, weights.pop(step - 2))
             return inner
 
         lax.fori_loop(0, cols // together, pixel_group, 0)
@@ -312,12 +337,13 @@
                 ).astype(jnp.bfloat16)
         for k in range(1, nt):
             back(k, s).start()
-        out_ref[:, t * span + s] = stage[t, s]
+        own(s).start()
         return carry
 
     lax.fori_loop(0, span, attend_unit, 0)
 
     def drain(s, carry):
+        own(s).wait()
         for k in range(1, nt):
             back(k, s).wait_recv()
             back(k, s).wait_send()
@@ -342,6 +368,7 @@
     span = rows // nt
     unit = cols * frames
     total = nt * frames
+    hbm = pl.BlockSpec(memory_space=pl.ANY)
     vmem = pl.BlockSpec(memory_space=pltpu.VMEM)
     bf16, f32, dma = jnp.bfloat16, jnp.float32, pltpu.SemaphoreType.DMA
     two = 2 if rows % 2 == 0 else 1
@@ -351,9 +378,11 @@
     out = pl.pallas_call(
         functools.partial(kernel, sizes),
         out_shape=jax.ShapeDtypeStruct(video.shape, bf16),
-        in_specs=[vmem] * 7,
-        out_specs=vmem,
+        in_specs=[hbm] * 3 + [vmem] * 2 + [hbm] * 2,
+        out_specs=hbm,
         scratch_shapes=[
+            pltpu.VMEM(video.shape, bf16), pltpu.VMEM(w_space.shape, bf16), pltpu.VMEM(w_time.shape, bf16),
+            pltpu.VMEM(w_qkv.shape, bf16), pltpu.VMEM(w_out.shape, bf16),
             pltpu.VMEM((rows + 2, cols + 2, frames, channels), bf16),
             pltpu.VMEM((rows, unit, channels), bf16),
             pltpu.VMEM((2, span, nt, cols, channels), bf16),
@@ -371,12 +400,12 @@
             pltpu.VMEM((nt, 8, channels), f32),
             pltpu.VMEM((nh, 8, channels), f32),
             pltpu.VMEM((nw, 8, channels), f32),
-            dma((len(STEPS),)), dma((len(STEPS),)), dma((2, span)), dma((2, span)),
+            dma((5,)), dma((span,)), dma((len(STEPS),)), dma((len(STEPS),)), dma((2, span)), dma((2, span)),
             dma((nt, span)), dma((nt, span)), dma((nt, span)), dma((nt, span)),
             dma((nt,)), dma((nt,)), dma((nh,)), dma((nh,)), dma((nw,)), dma((nw,)),
         ],
         compiler_params=pltpu.CompilerParams(
-            collective_id=0, has_side_effects=True, vmem_limit_bytes=52 * 1024 * 1024
+            collective_id=0, has_side_effects=True, vmem_limit_bytes=60 * 1024 * 1024
         ),
         cost_estimate=pl.CostEstimate(
             flops=2 * pixels * channels * channels * 20,

time: 88.2 us -> 83 us (0.941)
  local copies, waits for them, and re-layouts: 7.35 us -> 3.1 us
    unnamed x11 -> x1, local copies, waits for them, and re-layouts: 7.35 us -> 3.1 us
where the time goes in v4:
time: 83 us; the launch traced here: 82.9 us
  Pallas kernels  79.8 us (96%)
  local copies, waits for them, and re-layouts  3.1 us (4%)
    pallas_call x1, Pallas kernels, per_device(): pl.pallas_call(functools.partial(kernel, sizes), out_shape=jax.ShapeDtype...  79.8 us
    unnamed x1, local copies, waits for them, and re-layouts  3.1 us

profile of v4, /device:TPU:0, one launch (start us, length us, event | category | flops | bytes accessed | tf_op | source)
XLA Modules:
  0.0 82.9 jit_solution(18246306566018154603)
XLA Ops:
  0.0 79.8 %shard_map.73 = bf16[16,16,16,256]{3,2,1,0:T(8,128)(2,1)} custom-call(bf16[16,16,16,256]{3,2,1,0:T(8,128)(2,1)} %x_hbm.1, bf16[3,3,256,256]{3,2,1,0:T(8,128)(2,1)} %wsp_hbm.1, bf16[3,256,256]{2,1,0:T(8,128)(2,1)} %wt_hbm.1, f32[1,256]{1,0:T(1,128)} %bitcast.2, f32[1,256]{1,0:T(1,128)} %bitcast.3, bf16[256,768]{1,0:T(8,128)(2,1)} %wqkv_hbm.1, ...), custom_call_target="tpu_custom_call" | custom-call | flops 10737418240 | bytes 4194304 | tf_op jit(solution)/shard_map/pallas_call | solution.py:378
  79.8 3.1 %copy.9 = bf16[16,16,16,256]{3,2,1,0:T(8,128)(2,1)} copy(bf16[16,16,16,256]{3,2,1,0:T(8,128)(2,1)} %shard_map.73) | data formatting | bytes 4194304

commit v5 on v4

--- a/solution.py
+++ b/solution.py
@@ -170,7 +170,7 @@
     def spread(v):
         return jnp.broadcast_to(v[:, None, :], (block * cols, frames, channels)).reshape(block * unit, channels)
 
-    def time_round(s):
+    def time_round(s, send):
         for side, step in ((0, -1), (1, 1)):
             @pl.when(inside(t - step, nt))
             def _(side=side):
@@ -191,7 +191,8 @@
                 part = value[b * unit:(b + 1) * unit]
                 if k:
                     piece[k, s] = part
-                    forward(k, s).start()
+                    if send:
+                        forward(k, s).start()
                 else:
                     recv[t, s] = part
             wide = value.astype(jnp.float32)
@@ -200,16 +201,16 @@
 
     def both(s, carry):
         conv_round(s)
-        time_round(s - 1)
+        time_round(s - 1, True)
         return carry
 
     for load in loads[1:]:
         load.wait()
     conv_round(0)
     lax.fori_loop(1, span, both, 0)
-    time_round(span - 1)
-
-    def exchange(slots, size, me, device, send, arrive):
+    time_round(span - 1, False)
+
+    def exchange(slots, size, me, device, send, arrive, then=None):
         slots[me] = stat[...]
 
         def copy(k):
@@ -229,15 +230,22 @@
 
         for k in range(1, size):
             copy(k).start()
+        if then is not None:
+            then()
         for k in range(1, size):
             landed(k).wait_recv()
         stat[...] = jnp.sum(slots[...], axis=0)
         for k in range(1, size):
             copy(k).wait_send()
 
-    exchange(ex_t, nt, t, lambda o: (o, h, w), t_send, t_recv)
     exchange(ex_h, nh, h, lambda o: (t, o, w), h_send, h_recv)
     exchange(ex_w, nw, w, lambda o: (t, h, o), w_send, w_recv)
+
+    def send_last():
+        for k in range(1, nt):
+            forward(k, span - 1).start()
+
+    exchange(ex_t, nt, t, lambda o: (o, h, w), t_send, t_recv, send_last)
 
     cells = float(total * rows * nh * cols * nw * (channels // GROUPS))
     size = channels // GROUPS

time: 83 us -> 75.7 us (0.912)
  Pallas kernels: 79.8 us -> 72.5 us
    pallas_call x1, Pallas kernels: 79.8 us -> 72.5 us  [per_device(): pl.pallas_call(functools.partial(kernel, sizes), out_shape=jax.ShapeDtype...]
where the time goes in v5:
time: 75.7 us; the launch traced here: 75.6 us
  Pallas kernels  72.5 us (96%)
  local copies, waits for them, and re-layouts  3.1 us (4%)
    pallas_call x1, Pallas kernels, per_device(): pl.pallas_call(functools.partial(kernel, sizes), out_shape=jax.ShapeDtype...  72.5 us
    unnamed x1, local copies, waits for them, and re-layouts  3.1 us

profile of v5, /device:TPU:0, one launch (start us, length us, event | category | flops | bytes accessed | tf_op | source)
XLA Modules:
  0.0 75.6 jit_solution(7460233308698302680)
XLA Ops:
  0.0 72.5 %shard_map.73 = bf16[16,16,16,256]{3,2,1,0:T(8,128)(2,1)} custom-call(bf16[16,16,16,256]{3,2,1,0:T(8,128)(2,1)} %x_hbm.1, bf16[3,3,256,256]{3,2,1,0:T(8,128)(2,1)} %wsp_hbm.1, bf16[3,256,256]{2,1,0:T(8,128)(2,1)} %wt_hbm.1, f32[1,256]{1,0:T(1,128)} %bitcast.2, f32[1,256]{1,0:T(1,128)} %bitcast.3, bf16[256,768]{1,0:T(8,128)(2,1)} %wqkv_hbm.1, ...), custom_call_target="tpu_custom_call" | custom-call | flops 10737418240 | bytes 4194304 | tf_op jit(solution)/shard_map/pallas_call | solution.py:386
  72.5 3.1 %copy.9 = bf16[16,16,16,256]{3,2,1,0:T(8,128)(2,1)} copy(bf16[16,16,16,256]{3,2,1,0:T(8,128)(2,1)} %shard_map.73) | data formatting | bytes 4194304

commit v6 on v5

--- a/solution.py
+++ b/solution.py
@@ -83,7 +83,9 @@
                 ).astype(jnp.bfloat16)
         return carry
 
-    lax.fori_loop(0, rows // two, turn_in, 0)
+    ends = sorted({0, rows // two - 1})
+    for step in ends:
+        turn_in(step, 0)
     pl.semaphore_wait(barrier, count + (nt - 1) + (nh - 1) + (nw - 1))
 
     def span_of(step, size):
@@ -100,10 +102,16 @@
             device_id=(t, h + sign * dr, w + sign * dc), device_id_type=MESH,
         )
 
-    for index, (dr, dc) in enumerate(STEPS):
-        @pl.when(jnp.logical_and(inside(h + dr, nh), inside(w + dc, nw)))
-        def _(index=index):
-            halo(index, 1).start()
+    def send_halos(along):
+        for index, (dr, dc) in enumerate(STEPS):
+            if (dr != 0) == along:
+                @pl.when(jnp.logical_and(inside(h + dr, nh), inside(w + dc, nw)))
+                def _(index=index):
+                    halo(index, 1).start()
+
+    send_halos(True)
+    lax.fori_loop(1, rows // two - 1, turn_in, 0)
+    send_halos(False)
     for index, (dr, dc) in enumerate(STEPS):
         @pl.when(jnp.logical_not(jnp.logical_and(inside(h - dr, nh), inside(w - dc, nw))))
         def _(dr=dr, dc=dc):
@@ -368,6 +376,10 @@
         def _(side=side):
             for s in range(span):
                 edge(side, s, 1).wait_send()
+
+
+def copy_kernel(src_ref, dst_ref):
+    dst_ref[...] = src_ref[...]
 
 
 def per_device(sizes, video, w_space, w_time, norm_gain, norm_bias, w_qkv, w_out):
@@ -422,7 +434,15 @@
     )(
         video, w_space, w_time, norm_gain.reshape(1, channels), norm_bias.reshape(1, channels), w_qkv, w_out
     )
-    return out
+    part = frames // math.gcd(frames, 4)
+    block = pl.BlockSpec((part, rows, cols, channels), lambda i: (i, 0, 0, 0))
+    return pl.pallas_call(
+        copy_kernel,
+        out_shape=jax.ShapeDtypeStruct(video.shape, bf16),
+        grid=(frames // part,),
+        in_specs=[block],
+        out_specs=block,
+    )(out)
 
 
 def solution(mesh):

time: 75.7 us -> 75.3 us (level)
  local copies, waits for them, and re-layouts: 3.1 us -> 0 us
  Pallas kernels: 72.5 us -> 75.1 us
    pallas_call x0 -> x1, Pallas kernels: none -> 3.78 us  [per_device(): pl.pallas_call(copy_kernel, out_shape=jax.ShapeDtypeStruct(video.shape, b...]
    unnamed x1 -> x0, local copies, waits for them, and re-layouts: 3.1 us -> none
    pallas_call x1, Pallas kernels: 72.5 us -> 71.3 us  [per_device(): pl.pallas_call(functools.partial(kernel, sizes), out_shape=jax.ShapeDtype...]
where the time goes in v6:
time: 75.3 us; the launch traced here: 75.1 us
  Pallas kernels  75.1 us (100%)
    pallas_call x1, Pallas kernels, per_device(): pl.pallas_call(functools.partial(kernel, sizes), out_shape=jax.ShapeDtype...  71.3 us
    pallas_call x1, Pallas kernels, per_device(): pl.pallas_call(copy_kernel, out_shape=jax.ShapeDtypeStruct(video.shape, b...  3.78 us

profile of v6, /device:TPU:0, one launch (start us, length us, event | category | flops | bytes accessed | tf_op | source)
XLA Modules:
  0.0 75.1 jit_solution(8494133135272095968)
XLA Ops:
  0.0 71.3 %shard_map.73.src_ref = bf16[16,16,16,256]{3,2,1,0:T(8,128)(2,1)} custom-call(bf16[16,16,16,256]{3,2,1,0:T(8,128)(2,1)} %x_hbm.1, bf16[3,3,256,256]{3,2,1,0:T(8,128)(2,1)} %wsp_hbm.1, bf16[3,256,256]{2,1,0:T(8,128)(2,1)} %wt_hbm.1, f32[1,256]{1,0:T(1,128)} %bitcast.2, f32[1,256]{1,0:T(1,128)} %bitcast.3, bf16[256,768]{1,0:T(8,128)(2,1)} %wqkv_hbm.1, ...), custom_call_target="tpu_custom_call" | custom-call | flops 10737418240 | bytes 4194304 | tf_op jit(solution)/shard_map/pallas_call | solution.py:398
  71.3 3.8 %shard_map.74 = bf16[16,16,16,256]{3,2,1,0:T(8,128)(2,1)} custom-call(bf16[16,16,16,256]{3,2,1,0:T(8,128)(2,1)} %shard_map.73.src_ref), custom_call_target="tpu_custom_call" | custom-call | tf_op jit(solution)/shard_map/pallas_call | solution.py:439

commit v7 on v6

--- a/solution.py
+++ b/solution.py
@@ -376,10 +376,6 @@
         def _(side=side):
             for s in range(span):
                 edge(side, s, 1).wait_send()
-
-
-def copy_kernel(src_ref, dst_ref):
-    dst_ref[...] = src_ref[...]
 
 
 def per_device(sizes, video, w_space, w_time, norm_gain, norm_bias, w_qkv, w_out):
@@ -434,15 +430,7 @@
     )(
         video, w_space, w_time, norm_gain.reshape(1, channels), norm_bias.reshape(1, channels), w_qkv, w_out
     )
-    part = frames // math.gcd(frames, 4)
-    block = pl.BlockSpec((part, rows, cols, channels), lambda i: (i, 0, 0, 0))
-    return pl.pallas_call(
-        copy_kernel,
-        out_shape=jax.ShapeDtypeStruct(video.shape, bf16),
-        grid=(frames // part,),
-        in_specs=[block],
-        out_specs=block,
-    )(out)
+    return out
 
 
 def solution(mesh):

time: 75.3 us -> 74.6 us (level)
  Pallas kernels: 75.1 us -> 71.3 us
  local copies, waits for them, and re-layouts: 0 us -> 3.1 us
    pallas_call x1 -> x0, Pallas kernels: 3.78 us -> none  [per_device(): pl.pallas_call(copy_kernel, out_shape=jax.ShapeDtypeStruct(video.shape, b...]
    unnamed x0 -> x1, local copies, waits for them, and re-layouts: none -> 3.1 us
where the time goes in v7:
time: 74.6 us; the launch traced here: 74.4 us
  Pallas kernels  71.3 us (96%)
  local copies, waits for them, and re-layouts  3.1 us (4%)
    pallas_call x1, Pallas kernels, per_device(): pl.pallas_call(functools.partial(kernel, sizes), out_shape=jax.ShapeDtype...  71.3 us
    unnamed x1, local copies, waits for them, and re-layouts  3.1 us

profile of v7, /device:TPU:0, one launch (start us, length us, event | category | flops | bytes accessed | tf_op | source)
XLA Modules:
  0.0 74.4 jit_solution(1853328519232452204)
XLA Ops:
  0.0 71.3 %shard_map.73 = bf16[16,16,16,256]{3,2,1,0:T(8,128)(2,1)} custom-call(bf16[16,16,16,256]{3,2,1,0:T(8,128)(2,1)} %x_hbm.1, bf16[3,3,256,256]{3,2,1,0:T(8,128)(2,1)} %wsp_hbm.1, bf16[3,256,256]{2,1,0:T(8,128)(2,1)} %wt_hbm.1, f32[1,256]{1,0:T(1,128)} %bitcast.2, f32[1,256]{1,0:T(1,128)} %bitcast.3, bf16[256,768]{1,0:T(8,128)(2,1)} %wqkv_hbm.1, ...), custom_call_target="tpu_custom_call" | custom-call | flops 10737418240 | bytes 4194304 | tf_op jit(solution)/shard_map/pallas_call | solution.py:394
  71.3 3.1 %copy.9 = bf16[16,16,16,256]{3,2,1,0:T(8,128)(2,1)} copy(bf16[16,16,16,256]{3,2,1,0:T(8,128)(2,1)} %shard_map.73) | data formatting | bytes 4194304
